TPU v7x, 32 devices: a whole 2x2x4 slice. The times are simulated.
32 devices in a mesh: grp: 2 (over x), gx: 16 (over z, y, core).
Axes of the slice: x: 2, y: 2, z: 4, core: 2. Of those that a mesh axis runs over, the one named last changes fastest.
Arguments:
- e_forward: float32 [3, 256, 32, 256], P(None, ('grp', 'gx')), parts along dimension 1, may hold values from -6 to 6
- h_forward: float32 [3, 256, 32, 256], P(None, ('grp', 'gx')), parts along dimension 1, may hold values from -6 to 6
- p_forward: float32 [3, 256, 32, 256], P(None, ('grp', 'gx')), parts along dimension 1, may hold values from -6 to 6
- j_forward: float32 [3, 256, 32, 256], P(None, ('grp', 'gx')), parts along dimension 1, may hold values from -6 to 6
- e_adjoint: float32 [3, 256, 32, 256], P(None, ('grp', 'gx')), parts along dimension 1, may hold values from -6 to 6
- h_adjoint: float32 [3, 256, 32, 256], P(None, ('grp', 'gx')), parts along dimension 1, may hold values from -6 to 6
- p_adjoint: float32 [3, 256, 32, 256], P(None, ('grp', 'gx')), parts along dimension 1, may hold values from -6 to 6
- j_adjoint: float32 [3, 256, 32, 256], P(None, ('grp', 'gx')), parts along dimension 1, may hold values from -6 to 6
- design: float32 [32, 32, 256], P(('grp', 'gx')), parts along dimension 0, may hold values from 0 to 1
- source_amp: float32 [32, 3], P('grp'), parts along dimension 0, may hold values from -6 to 6
- source_cell: int32 [32], P('grp'), parts along dimension 0, may hold values from 0 to 1048575
- monitor_cell: int32 [32], P('grp'), parts along dimension 0, may hold values from 0 to 1048575
- slab_start: int32 [2], P('grp'), parts along dimension 0, may hold values from 8 to 15
- radius: int32 [2], P('grp'), parts along dimension 0, may hold values from 1 to 4
Outputs:
- e_forward_next: float32 [3, 256, 32, 256], P(None, ('grp', 'gx')), parts along dimension 1
- h_forward_next: float32 [3, 256, 32, 256], P(None, ('grp', 'gx')), parts along dimension 1
- e_adjoint_next: float32 [3, 256, 32, 256], P(None, ('grp', 'gx')), parts along dimension 1
- h_adjoint_next: float32 [3, 256, 32, 256], P(None, ('grp', 'gx')), parts along dimension 1
- design_grad: float32 [32, 32, 256], P(('grp', 'gx')), parts along dimension 0
There are 2 independent parts, one for each index of `grp`. A program takes and returns all parts, laid end to end along the dimension named above; each array names one. Nothing has to cross between parts.
Inputs may be any that keep to these rules, and one draw needn't show every extreme that they name: `slab_start`: the slab begins within planes 8 to 15 of the grid.
All inputs are finite; a program needn't handle non-finite values.
Results may differ from a plain program's by a relative error of at most 0.0003.
Values sent between devices are 32-bit elements; how exact they have to be, the bound alone decides.
A program may use at most 128 MiB of HBM per device.

v0:
```python
import jax
import jax.numpy as jnp
from jax import lax
from jax.sharding import PartitionSpec as P

DT = 0.5
EPS_RANGE = 10.0
STRENGTH_BASE = 0.5
STRENGTH_RANGE = 3.0
DAMPING = 0.2
GAIN_FIELD = 0.25
HIGH = lax.Precision.HIGHEST


def passed_along(block, axis, distance):
    devices = range(lax.axis_size(axis))
    route = [(i - distance, i) for i in devices if i - distance in devices]
    return lax.ppermute(block, axis, route)


def band_matrix(count, radius):
    rows = jnp.arange(count, dtype=jnp.int32)
    dist = jnp.abs(rows[:, None] - rows[None, :])
    weights = jnp.maximum(radius + 1 - dist, 0).astype(jnp.float32)
    return weights / jnp.sum(weights, axis=1, keepdims=True)


def ahead(field, axis):
    count = field.shape[axis]
    rest = lax.slice_in_dim(field, 1, count, axis=axis)
    return jnp.concatenate([rest, jnp.zeros_like(lax.slice_in_dim(field, 0, 1, axis=axis))], axis)


def behind(field, axis):
    count = field.shape[axis]
    rest = lax.slice_in_dim(field, 0, count - 1, axis=axis)
    return jnp.concatenate([jnp.zeros_like(lax.slice_in_dim(field, 0, 1, axis=axis)), rest], axis)


def update_h(efield, hfield, upper):
    ex, ey, ez = (efield[0], efield[1], efield[2])
    ex_next = jnp.concatenate([ex[1:], upper[0][None]], 0)
    ey_next = jnp.concatenate([ey[1:], upper[1][None]], 0)
    curl_x = ahead(ez, 2) - ez - (ey_next - ey)
    curl_y = ex_next - ex - (ahead(ez, 1) - ez)
    curl_z = ahead(ey, 1) - ey - (ahead(ex, 2) - ex)
    return hfield - DT * jnp.stack([curl_x, curl_y, curl_z])


def update_e(efield, hnext, lower, jnext, permittivity, drive):
    hx, hy, hz = (hnext[0], hnext[1], hnext[2])
    hx_prev = jnp.concatenate([lower[0][None], hx[:-1]], 0)
    hy_prev = jnp.concatenate([lower[1][None], hy[:-1]], 0)
    curl_x = hz - behind(hz, 2) - (hy - hy_prev)
    curl_y = hx - hx_prev - (hz - behind(hz, 1))
    curl_z = hy - behind(hy, 1) - (hx - behind(hx, 2))
    curl = jnp.stack([curl_x, curl_y, curl_z])
    return efield + (DT / permittivity)[None] * (curl - jnext + drive)


def update_j(jfield, pfield, efield, strength):
    return ((1.0 - DAMPING * DT / 2.0) * jfield + DT * (strength[None] * efield - pfield)) / (
        1.0 + DAMPING * DT / 2.0
    )


def smooth(wx, wy, planes):
    inner = jnp.einsum("ax,zxy->zay", wx, planes, precision=HIGH)
    return jnp.einsum("zay,by->zab", inner, wy, precision=HIGH)


def smooth_adjoint(wx, wy, planes):
    inner = jnp.einsum("ax,zab->zxb", wx, planes, precision=HIGH)
    return jnp.einsum("zxb,by->zxy", inner, wy, precision=HIGH)


def locate(cells, first, depth, width_x, width_y):
    zz = cells // (width_x * width_y)
    rest = cells % (width_x * width_y)
    local = zz - first
    inside = ((local >= 0) & (local < depth)).astype(jnp.float32)
    return (jnp.clip(local, 0, depth - 1), rest // width_y, rest % width_y, inside)


def body(
    e_forward,
    h_forward,
    p_forward,
    j_forward,
    e_adjoint,
    h_adjoint,
    p_adjoint,
    j_adjoint,
    design,
    source_amp,
    source_cell,
    monitor_cell,
    slab_start,
    radius,
):
    count = lax.axis_size("gx")
    index = lax.axis_index("gx")
    depth, width_x, width_y = (e_forward.shape[1], e_forward.shape[2], e_forward.shape[3])
    start = slab_start[0]
    wx = band_matrix(width_x, radius[0])
    wy = band_matrix(width_y, radius[0])
    planes = index * depth + jnp.arange(depth, dtype=jnp.int32) - start
    select = (planes[:, None] == jnp.arange(count, dtype=jnp.int32)[None, :]).astype(jnp.float32)
    upper = passed_along(
        jnp.stack([e_forward[0, 0], e_forward[1, 0], e_adjoint[0, 0], e_adjoint[1, 0]]), "gx", -1
    )
    hf = update_h(e_forward, h_forward, upper[0:2])
    ha = update_h(e_adjoint, h_adjoint, upper[2:4])
    owned = smooth(wx, wy, design)
    holder = (start + index) // depth
    target = (jnp.arange(count, dtype=jnp.int32) == holder).astype(jnp.float32)
    slots = target[:, None, None] * owned
    arrived = lax.all_to_all(slots, "gx", split_axis=0, concat_axis=0, tiled=True)
    density = jnp.einsum("lo,oxy->lxy", select, arrived, precision=HIGH)
    permittivity = 1.0 + EPS_RANGE * density
    strength = STRENGTH_BASE + STRENGTH_RANGE * density
    lower = passed_along(jnp.stack([hf[0, -1], hf[1, -1], ha[0, -1], ha[1, -1]]), "gx", 1)
    zs, xs, ys, inside_s = locate(source_cell, index * depth, depth, width_x, width_y)
    drive = (
        jnp.zeros((3, depth, width_x, width_y), jnp.float32)
        .at[:, zs, xs, ys]
        .add(source_amp.T * inside_s[None, :])
    )
    zm, xm, ym, inside_m = locate(monitor_cell, index * depth, depth, width_x, width_y)
    probe = e_forward[:, zm, xm, ym] * inside_m[None, :]
    drive_adj = jnp.zeros((3, depth, width_x, width_y), jnp.float32).at[:, zm, xm, ym].add(probe)
    jf = update_j(j_forward, p_forward, e_forward, strength)
    ja = update_j(j_adjoint, p_adjoint, e_adjoint, strength)
    ef = update_e(e_forward, hf, lower[0:2], jf, permittivity, drive)
    ea = update_e(e_adjoint, ha, lower[2:4], ja, permittivity, drive_adj)
    intersection = jnp.sum(ea * (ef - e_forward + GAIN_FIELD * ef), axis=0)
    returned = jnp.einsum("lo,lxy->oxy", select, intersection, precision=HIGH)
    arrived_back = lax.all_to_all(returned, "gx", split_axis=0, concat_axis=0, tiled=True)
    own_intersection = jnp.sum(arrived_back, axis=0, keepdims=True)
    design_grad = smooth_adjoint(wx, wy, own_intersection)
    return (ef, hf, ea, ha, design_grad)


def solution(mesh):
    return jax.shard_map(
        body,
        mesh=mesh,
        in_specs=(
            P(None, ("grp", "gx"), None, None),
            P(None, ("grp", "gx"), None, None),
            P(None, ("grp", "gx"), None, None),
            P(None, ("grp", "gx"), None, None),
            P(None, ("grp", "gx"), None, None),
            P(None, ("grp", "gx"), None, None),
            P(None, ("grp", "gx"), None, None),
            P(None, ("grp", "gx"), None, None),
            P(("grp", "gx"), None, None),
            P("grp", None),
            P("grp"),
            P("grp"),
            P("grp"),
            P("grp"),
        ),
        out_specs=(
            P(None, ("grp", "gx"), None, None),
            P(None, ("grp", "gx"), None, None),
            P(None, ("grp", "gx"), None, None),
            P(None, ("grp", "gx"), None, None),
            P(("grp", "gx"), None, None),
        ),
        check_vma=False,
    )
```

profile of v0, /device:TPU:0, one launch (start us, length us, event | category | flops | bytes accessed | tf_op | source)
XLA Modules:
  0.0 170.5 jit_solution(10110285703534453992)
XLA Ops:
  2.3 1.3 collective-permute-start
  6.8 8.8 %all-to-all-start = ((f32[16,32,256]{2,1,0:T(8,128)}), f32[16,32,256]{2,1,0:T(8,128)}, u32[]{:S(2)}, u32[]{:S(2)}) async-start(f32[16,32,256]{2,1,0:T(8,128)} %broadcast_multiply_fusion), calls=%async_computation | async-start | bytes 1048576 | tf_op jit(solution)/shard_map/all_to_all | solution.py:118
  15.6 1.9 %slice_bitcast_fusion.17 = (f32[7,32,256]{2,1,0:T(8,128)}, f32[7,32,256]{2,1,0:T(8,128)}) fusion(f32[3,8,32,256]{3,2,1,0:T(8,128)} %param.18), kind=kLoop, calls=%fused_computation.69 | loop fusion | bytes 917504 | tf_op jit(solution)/shard_map/slice | solution.py:43
  17.5 1.9 %slice_bitcast_fusion.19 = (f32[7,32,256]{2,1,0:T(8,128)}, f32[7,32,256]{2,1,0:T(8,128)}) fusion(f32[3,8,32,256]{3,2,1,0:T(8,128)} %param.14), kind=kLoop, calls=%fused_computation.71 | loop fusion | bytes 917504 | tf_op jit(solution)/shard_map/slice | solution.py:43
  19.3 2.0 %slice_bitcast_fusion.8 = (f32[8,32,256]{2,1,0:T(8,128)S(1)}, f32[8,32,256]{2,1,0:T(8,128)}, f32[8,32,256]{2,1,0:T(8,128)}) fusion(f32[3,8,32,256]{3,2,1,0:T(8,128)} %param.18), kind=kLoop, calls=%fused_computation.54 | loop fusion | bytes 1572864 | tf_op jit(solution)/shard_map/squeeze | solution.py:41
  21.3 1.9 %slice_bitcast_fusion.11 = (f32[8,32,256]{2,1,0:T(8,128)S(1)}, f32[8,32,256]{2,1,0:T(8,128)}, f32[8,32,256]{2,1,0:T(8,128)S(1)}) fusion(f32[3,8,32,256]{3,2,1,0:T(8,128)} %param.14), kind=kLoop, calls=%fused_computation.58 | loop fusion | bytes 1572864 | tf_op jit(solution)/shard_map/squeeze | solution.py:41
  23.2 17.6 %copy.649 = f32[3,8,32,256]{0,3,2,1:T(8,128)} copy(f32[3,8,32,256]{3,2,1,0:T(8,128)} %param.14) | data formatting | bytes 1572864 | tf_op args[0]
  40.8 1.3 gather_fusion
  46.7 1.3 fusion.9
  47.9 1.2 fusion.1
  49.3 1.4 fusion.5
  50.7 1.2 fusion
  52.1 2.3 %collective-permute-start.1 = (f32[4,32,256]{2,1,0:T(8,128)S(1)}, f32[4,32,256]{2,1,0:T(8,128)S(1)}, u32[]{:S(2)}, u32[]{:S(2)}) collective-permute-start(f32[4,32,256]{2,1,0:T(8,128)S(1)} %pad_maximum_fusion.1), channel_id=1, source_target_pairs={{0,1},{1,2},{2,3},{3,4},{4,5},{5,6},{6,7},{7,8},{8,9},{9,10},{10,1... | collective-permute-start | bytes 393224 | tf_op jit(solution)/shard_map/ppermute | solution.py:18
  56.3 1.1 fusion.13
  57.5 1.7 add_divide_fusion
  60.0 4.2 %maximum_subtract_fusion = (f32[3,8,32,256]{3,2,1,0:T(8,128)}, f32[3,8,32,256]{3,2,1,0:T(8,128)}) fusion(f32[1,8,32,256]{3,2,1,0:T(8,128)} %get-tuple-element.109, f32[1,8,32,256]{3,2,1,0:T(8,128)} %get-tuple-element.110, f32[1,8,32,256]{3,2,1,0:T(8,128)} %get-tuple-element.108, f32[3,8,32,256]{3,2,1,0:T(8,128)} %param.16, ...), kind=kLoop, calls=%fused_computation.9 | loop fusion | flops 3538944 | bytes 8126464 | tf_op jit(solution)/shard_map/sub | solution.py:58
  64.2 17.6 %copy.646 = f32[3,8,32,256]{0,3,2,1:T(8,128)} copy(f32[3,8,32,256]{3,2,1,0:T(8,128)} %get-tuple-element.148) | data formatting | bytes 1572864 | tf_op jit(solution)/shard_map/sub | solution.py:58
  81.8 2.2 %scatter_fusion = f32[3,8,32,256]{0,3,2,1:T(8,128)} fusion(f32[3,8,32,256]{0,3,2,1:T(8,128)} %copy.646, s32[16]{0:T(128)S(1)} %fusion.52, f32[16,3]{1,0:T(8,128)S(1)} %copy.647), kind=kCustom, calls=%fused_computation.1 | custom fusion | flops 48 | bytes 768 | tf_op jit(solution)/shard_map/scatter-add | solution.py:127
  84.0 20.2 %copy.648 = f32[3,8,32,256]{3,2,1,0:T(8,128)} copy(f32[3,8,32,256]{0,3,2,1:T(8,128)} %scatter_fusion) | data formatting | bytes 1572864 | tf_op jit(solution)/shard_map/scatter-add | solution.py:127
  104.2 17.7 %copy.650 = f32[3,8,32,256]{0,3,2,1:T(8,128)} copy(f32[3,8,32,256]{3,2,1,0:T(8,128)} %get-tuple-element.149) | data formatting | bytes 1572864 | tf_op jit(solution)/shard_map/sub | solution.py:58
  121.9 2.2 %scatter_fusion.1 = f32[3,8,32,256]{0,3,2,1:T(8,128)} fusion(f32[3,8,32,256]{0,3,2,1:T(8,128)} %copy.650, s32[16]{0:T(128)S(1)} %get-tuple-element.161, f32[16,3]{1,0:T(8,128)S(1)} %broadcast_multiply_fusion.1), kind=kCustom, calls=%fused_computation.2 | custom fusion | flops 48 | bytes 768 | tf_op jit(solution)/shard_map/scatter-add | solution.py:131
  124.1 19.5 %copy.651 = f32[3,8,32,256]{3,2,1,0:T(8,128)S(1)} copy(f32[3,8,32,256]{0,3,2,1:T(8,128)} %scatter_fusion.1) | data formatting | bytes 1572864 | tf_op jit(solution)/shard_map/scatter-add | solution.py:131
  143.5 1.6 multiply_reduce_fusion
  145.9 23.3 %all_to_all.10 = f32[16,32,256]{2,1,0:T(8,128)S(1)} all-to-all(f32[16,32,256]{2,1,0:T(8,128)S(1)} %copy.654), channel_id=1, replica_groups=mesh['grp'=2,'gx'=16] {'gx'}, dimensions={0} | all-to-all | bytes 1048576 | tf_op jit(solution)/shard_map/all_to_all | solution.py:138
  (65 shorter events, 13.1 us)
Async XLA Ops:
  0.6 4.6 %copy-start = (f32[1,32,256]{2,1,0:T(8,128)S(1)}, f32[1,32,256]{2,1,0:T(8,128)}, u32[]{:S(2)}) copy-start(f32[1,32,256]{2,1,0:T(8,128)} %param.22) | copy-start | bytes 98308
  0.6 48.7 %copy-start.2 = (f32[3,8,32,256]{3,2,1,0:T(8,128)S(1)}, f32[3,8,32,256]{3,2,1,0:T(8,128)}, u32[]{:S(2)}) copy-start(f32[3,8,32,256]{3,2,1,0:T(8,128)} %param.14) | copy-start | bytes 2359300
  0.7 46.0 %copy-start.3 = (f32[3,8,32,256]{3,2,1,0:T(8,128)S(1)}, f32[3,8,32,256]{3,2,1,0:T(8,128)}, u32[]{:S(2)}) copy-start(f32[3,8,32,256]{3,2,1,0:T(8,128)} %param.18) | copy-start | bytes 2359300
  0.7 40.1 %copy-start.10 = (s32[16]{0:T(128)S(1)}, s32[16]{0:T(128)}, u32[]{:S(2)}) copy-start(s32[16]{0:T(128)} %param.24) | copy-start | bytes 196
  0.7 40.1 %copy-start.9 = (s32[16]{0:T(128)S(1)}, s32[16]{0:T(128)}, u32[]{:S(2)}) copy-start(s32[16]{0:T(128)} %param.25) | copy-start | bytes 196
  0.7 40.1 %copy-start.8 = (f32[16,3]{0,1:T(4,128)S(1)}, f32[16,3]{0,1:T(4,128)}, u32[]{:S(2)}) copy-start(f32[16,3]{0,1:T(4,128)} %param.23) | copy-start | bytes 580
  2.3 43.6 %collective-permute-start = (f32[4,32,256]{2,1,0:T(8,128)}, f32[4,32,256]{2,1,0:T(8,128)}, u32[]{:S(2)}, u32[]{:S(2)}) collective-permute-start(f32[4,32,256]{2,1,0:T(8,128)} %pad_maximum_fusion), channel_id=1, source_target_pairs={{1,0},{2,1},{3,2},{4,3},{5,4},{6,5},{7,6},{8,7},{9,8},{10,9},{11,1... | collective-permute-start | bytes 393224 | tf_op jit(solution)/shard_map/ppermute | solution.py:18
  6.8 50.7 %all-to-all-start = ((f32[16,32,256]{2,1,0:T(8,128)}), f32[16,32,256]{2,1,0:T(8,128)}, u32[]{:S(2)}, u32[]{:S(2)}) async-start(f32[16,32,256]{2,1,0:T(8,128)} %broadcast_multiply_fusion), calls=%async_computation | async-start | bytes 1048576 | tf_op jit(solution)/shard_map/all_to_all | solution.py:118
  49.2 55.0 %copy-start.4 = (f32[3,8,32,256]{3,2,1,0:T(8,128)}, f32[3,8,32,256]{3,2,1,0:T(8,128)S(1)}, u32[]{:S(2)}) copy-start(f32[3,8,32,256]{3,2,1,0:T(8,128)S(1)} %fusion.1) | copy-start | bytes 2359300
  52.0 52.2 %copy-start.5 = (f32[3,8,32,256]{3,2,1,0:T(8,128)}, f32[3,8,32,256]{3,2,1,0:T(8,128)S(1)}, u32[]{:S(2)}) copy-start(f32[3,8,32,256]{3,2,1,0:T(8,128)S(1)} %fusion) | copy-start | bytes 2359300
  52.1 3.2 %collective-permute-start.1 = (f32[4,32,256]{2,1,0:T(8,128)S(1)}, f32[4,32,256]{2,1,0:T(8,128)S(1)}, u32[]{:S(2)}, u32[]{:S(2)}) collective-permute-start(f32[4,32,256]{2,1,0:T(8,128)S(1)} %pad_maximum_fusion.1), channel_id=1, source_target_pairs={{0,1},{1,2},{2,3},{3,4},{4,5},{5,6},{6,7},{7,8},{8,9},{9,10},{10,1... | collective-permute-start | bytes 393224 | tf_op jit(solution)/shard_map/ppermute | solution.py:18
  104.2 66.4 %copy-start.1 = (f32[1,32,256]{2,1,0:T(8,128)S(1)}, f32[1,32,256]{2,1,0:T(8,128)}, u32[]{:S(2)}) copy-start(f32[1,32,256]{2,1,0:T(8,128)} %param.22) | copy-start | bytes 98308
  104.2 39.3 %copy-start.6 = (f32[3,8,32,256]{3,2,1,0:T(8,128)S(1)}, f32[3,8,32,256]{3,2,1,0:T(8,128)}, u32[]{:S(2)}) copy-start(f32[3,8,32,256]{3,2,1,0:T(8,128)} %copy.648) | copy-start | bytes 2359300
  104.2 39.3 %copy-start.7 = (f32[8,32,256]{2,1,0:T(8,128)S(1)}, f32[8,32,256]{2,1,0:T(8,128)}, u32[]{:S(2)}) copy-start(f32[8,32,256]{2,1,0:T(8,128)} %copy.644) | copy-start | bytes 786436
where the time goes:
time: 174 us; the launch traced here: 171 us
  local copies, waits for them, and re-layouts  108 us (62%)
  blocking collectives  23.3 us (13%)
  other arithmetic  19.4 us (11%)
  starting transfers between devices  12.4 us (7%)
  matrix products  4.06 us (2%)
  between operations  2.36 us (1%)
    sub x2, local copies, waits for them, and re-layouts, update_e(): return efield + (DT / permittivity)[None] * (curl - jnext + drive)  35.2 us
    all_to_all x1, blocking collectives, body(): lax.all_to_all(returned, 'gx', split_axis=0, concat_axis=0, tiled=True)  23.3 us
    scatter-add x1, local copies, waits for them, and re-layouts, body(): drive = jnp.zeros((3, depth, width_x, width_y), jnp.float32).at[:, zs, xs...  20.2 us
    scatter-add x1, local copies, waits for them, and re-layouts, body(): jnp.zeros((3, depth, width_x, width_y), jnp.float32).at[:, zm, xm, ym]  19.5 us
    unnamed x23, local copies, waits for them, and re-layouts  17.6 us
    all_to_all x1, starting transfers between devices, body(): lax.all_to_all(slots, 'gx', split_axis=0, concat_axis=0, tiled=True)  8.81 us
    slice x3, local copies, waits for them, and re-layouts, update_h(): ey_next = jnp.concatenate([ey[1:], upper[1][None]], 0)  4.59 us
    sub x1, other arithmetic, update_e(): return efield + (DT / permittivity)[None] * (curl - jnext + drive)  4.2 us
  transfers between devices with their start and end apart: 3, of which 1 were waited for; matrix products, arithmetic and copies ran while one was open for 24% of the time, Pallas kernels for 0%

commit v1 on v0

v1 whole, which is shorter than its diff:
```python
import functools

import jax
import jax.numpy as jnp
from jax import lax
from jax.experimental import pallas as pl
from jax.experimental.pallas import tpu as pltpu
from jax.sharding import PartitionSpec as P

DT = 0.5
EPS_RANGE = 10.0
STRENGTH_BASE = 0.5
STRENGTH_RANGE = 3.0
DAMPING = 0.2
GAIN_FIELD = 0.25
MESH = pl.DeviceIdType.MESH
F32 = jnp.float32
BF16 = jnp.bfloat16
ANY = pl.BlockSpec(memory_space=pl.ANY)
SMEM = pl.BlockSpec(memory_space=pltpu.SMEM)
VMEM = pl.BlockSpec(memory_space=pltpu.VMEM)


def slot_range(me, n, depth):
    base = depth * (me - 1) - (depth - 1)
    return base, jnp.maximum(base, 0), jnp.minimum(base + 2 * depth - 1, n)


def holders(me, depth):
    first = me // depth + 1
    return first, first + 1, me % depth


def ahead(v, axis):
    size = v.shape[axis]
    pos = lax.broadcasted_iota(jnp.int32, v.shape, axis)
    return jnp.where(pos == size - 1, 0.0, pltpu.roll(v, size - 1, axis))


def behind(v, axis):
    pos = lax.broadcasted_iota(jnp.int32, v.shape, axis)
    return jnp.where(pos == 0, 0.0, pltpu.roll(v, 1, axis))


def triangle(size, radius):
    a = lax.broadcasted_iota(jnp.int32, (size, size), 0)
    b = lax.broadcasted_iota(jnp.int32, (size, size), 1)
    return jnp.maximum(radius + 1 - jnp.abs(a - b), 0).astype(F32).astype(BF16)


def row_sums(shape, axis, radius):
    pos = lax.broadcasted_iota(jnp.int32, shape, axis)
    low = jnp.maximum(radius - pos, 0)
    high = jnp.maximum(radius - (shape[axis] - 1 - pos), 0)
    whole = (radius + 1) * (radius + 1)
    low, high = low.astype(F32), high.astype(F32)
    return whole.astype(F32) - 0.5 * (low * (low + 1.0) + high * (high + 1.0))


def halves(v):
    big = v.astype(BF16)
    return big, (v - big.astype(F32)).astype(BF16)


def band_product(plane, radius):
    nx, ny = plane.shape
    tx, ty = triangle(nx, radius), triangle(ny, radius)
    big, small = halves(plane)
    both = jnp.dot(jnp.concatenate([big, small], 0), ty, preferred_element_type=F32)
    big, small = halves(both[:nx] + both[nx:])
    return jnp.dot(tx, big, preferred_element_type=F32) + jnp.dot(
        tx, small, preferred_element_type=F32
    )


def inverse_sums(shape, radius):
    return 1.0 / (row_sums(shape, 0, radius) * row_sums(shape, 1, radius))


def exchange_kernel(
    n,
    radius_ref,
    design_ref,
    ef,
    ea,
    hf,
    ha,
    below_ref,
    above_ref,
    slots_ref,
    eb,
    hb,
    part,
    rho,
    load_sem,
    send_sem,
    up_send,
    up_recv,
    down_send,
    down_recv,
    slot_recv,
    self_sem,
):
    me = lax.axis_index("gx")
    depth = ef.shape[1]
    loads = []
    for r, (e, h) in enumerate(((ef, hf), (ea, ha))):
        loads.append(pltpu.make_async_copy(e.at[:, depth - 1], eb.at[r], load_sem.at[r, 0]))
        loads.append(pltpu.make_async_copy(h.at[0:2, depth - 1], hb.at[r], load_sem.at[r, 1]))
    for load in loads:
        load.start()

    barrier = pltpu.get_barrier_semaphore()

    @pl.loop(1, n)
    def _(k):
        pl.semaphore_signal(
            barrier, inc=1, device_id={"gx": lax.rem(me + k, n)}, device_id_type=MESH
        )

    radius = radius_ref[0]
    plane = design_ref[0]
    rho[...] = band_product(plane, radius) * inverse_sums(plane.shape, radius)
    pl.semaphore_wait(barrier, n - 1)

    first, second, shift = holders(me, depth)

    def to_holder(which, holder):
        slot = me - (depth * (holder - 1) - (depth - 1))
        return pltpu.make_async_remote_copy(
            src_ref=rho,
            dst_ref=slots_ref.at[slot],
            send_sem=send_sem.at[which],
            recv_sem=slot_recv.at[slot],
            device_id={"gx": holder},
            device_id_type=MESH,
        )

    def to_self(holder):
        slot = me - (depth * (holder - 1) - (depth - 1))
        return pltpu.make_async_copy(rho, slots_ref.at[slot], self_sem)

    def each_holder(remote, local):
        for which, holder, used in ((0, first, shift >= 0), (1, second, shift != 0)):
            pl.when(used & (holder != me))(functools.partial(remote, which, holder))
            pl.when(used & (holder == me))(functools.partial(local, holder))

    def to_below(r, e):
        return pltpu.make_async_remote_copy(
            src_ref=e.at[0:2, 0],
            dst_ref=above_ref.at[r],
            send_sem=down_send.at[r],
            recv_sem=down_recv.at[r],
            device_id={"gx": me - 1},
            device_id_type=MESH,
        )

    def to_above():
        return pltpu.make_async_remote_copy(
            src_ref=part,
            dst_ref=below_ref,
            send_sem=up_send,
            recv_sem=up_recv,
            device_id={"gx": me + 1},
            device_id_type=MESH,
        )

    each_holder(
        lambda which, holder: to_holder(which, holder).start(),
        lambda holder: to_self(holder).start(),
    )

    @pl.when(me > 0)
    def _():
        to_below(0, ef).start()
        to_below(1, ea).start()

    for load in loads:
        load.wait()
    for r in range(2):
        ex, ey, ez = eb[r, 0], eb[r, 1], eb[r, 2]
        part[r, 0] = hb[r, 0] - DT * (ahead(ez, 1) - ez + ey)
        part[r, 1] = hb[r, 1] + DT * (ex + (ahead(ez, 0) - ez))

    @pl.when(me < n - 1)
    def _():
        to_above().start()

    each_holder(
        lambda which, holder: to_holder(which, holder).wait_send(),
        lambda holder: to_self(holder).wait(),
    )

    @pl.when(me > 0)
    def _():
        to_below(0, ef).wait_send()
        to_below(1, ea).wait_send()
        to_above().wait_recv()

    @pl.when(me < n - 1)
    def _():
        to_above().wait_send()
        to_below(0, ef).wait_recv()
        to_below(1, ea).wait_recv()

    base, low, high = slot_range(me, n, depth)

    @pl.loop(low, high)
    def _(owner):
        @pl.when(owner != me)
        def _():
            pltpu.make_async_remote_copy(
                src_ref=rho,
                dst_ref=slots_ref.at[owner - base],
                send_sem=send_sem.at[0],
                recv_sem=slot_recv.at[owner - base],
                device_id={"gx": owner},
                device_id_type=MESH,
            ).wait_recv()


def step_kernel(
    n,
    start_ref,
    amp_ref,
    source_ref,
    monitor_ref,
    ef_in,
    hf_in,
    pf_in,
    jf_in,
    ea_in,
    ha_in,
    pa_in,
    ja_in,
    below_in,
    above_in,
    slots_in,
    ef_out,
    hf_out,
    ea_out,
    ha_out,
    product_out,
    e,
    h,
    p,
    j,
    below,
    above,
    rho,
    drive,
    seen,
    product,
    en,
    hn,
    in_sem,
    out_sem,
    side_sem,
):
    me = lax.axis_index("gx")
    _, _, depth, nx, ny = e.shape
    start = start_ref[0]
    first_slot = 2 * depth - 1 - start
    sides = [
        pltpu.make_async_copy(below_in, below, side_sem.at[0]),
        pltpu.make_async_copy(slots_in.at[pl.ds(first_slot, depth)], rho, side_sem.at[1]),
        pltpu.make_async_copy(above_in, above, side_sem.at[2]),
    ]
    loads = {}
    pairs = ((e, ef_in, ea_in), (h, hf_in, ha_in), (j, jf_in, ja_in), (p, pf_in, pa_in))
    for l in range(depth):
        for k, (ref, *sources) in enumerate(pairs):
            for r, source in enumerate(sources):
                loads[k, l, r] = pltpu.make_async_copy(
                    source.at[:, l], ref.at[r, :, l], in_sem.at[k, l, r]
                )
    for r in range(2):
        loads[0, 0, r].start()
    for l in range(depth):
        for r in range(2):
            if l + 1 < depth:
                loads[0, l + 1, r].start()
            for k in (1, 2, 3):
                loads[k, l, r].start()
        if l == 0:
            sides[0].start()
            sides[1].start()
    sides[2].start()

    drive[...] = jnp.zeros_like(drive)
    seen[...] = jnp.zeros_like(seen)
    first_row = me * (depth * nx)
    lanes = lax.broadcasted_iota(jnp.int32, (1, ny), 1)

    @pl.loop(0, source_ref.shape[0])
    def _(s):
        cell = source_ref[s]
        row = cell // ny - first_row

        @pl.when((row >= 0) & (row < depth * nx))
        def _():
            hit = lanes == cell % ny
            for c in range(3):
                drive[c, pl.ds(row, 1), :] += jnp.where(hit, amp_ref[c, s], 0.0)

    @pl.loop(0, monitor_ref.shape[0])
    def _(s):
        cell = monitor_ref[s]
        row = cell // ny - first_row

        @pl.when((row >= 0) & (row < depth * nx))
        def _():
            seen[pl.ds(row, 1), :] += jnp.where(lanes == cell % ny, 1.0, 0.0)

    stores = []

    def store(source, dst, *index):
        copy = pltpu.make_async_copy(source, dst, out_sem.at[*index])
        copy.start()
        stores.append(copy)

    for r in range(2):
        loads[0, 0, r].wait()
    for l in range(depth):
        for r in range(2):
            if l + 1 < depth:
                loads[0, l + 1, r].wait()
            for k in (1, 2, 3):
                loads[k, l, r].wait()
        if l == 0:
            sides[0].wait()
            sides[1].wait()
        if l == depth - 1:
            sides[2].wait()
        owner = me * depth + l - start
        density = jnp.where((owner >= 0) & (owner < n), rho[l], 0.0)
        scale = DT / (1.0 + EPS_RANGE * density)
        strength = STRENGTH_BASE + STRENGTH_RANGE * density
        rows = pl.ds(l * nx, nx)
        old = new = None
        for r in range(2):
            ex, ey, ez = e[r, 0, l], e[r, 1, l], e[r, 2, l]
            if l + 1 < depth:
                ex_up, ey_up = e[r, 0, l + 1], e[r, 1, l + 1]
            else:
                ex_up = jnp.where(me < n - 1, above[r, 0], 0.0)
                ey_up = jnp.where(me < n - 1, above[r, 1], 0.0)
            hx = h[r, 0, l] - DT * ((ahead(ez, 1) - ez) - (ey_up - ey))
            hy = h[r, 1, l] - DT * ((ex_up - ex) - (ahead(ez, 0) - ez))
            hz = h[r, 2, l] - DT * ((ahead(ey, 0) - ey) - (ahead(ex, 1) - ex))
            hn[r, 0, l] = hx
            hn[r, 1, l] = hy
            hn[r, 2, l] = hz
            store(hn.at[r, :, l], (hf_out, ha_out)[r].at[:, l], 1, l, r)
            if l:
                hx_low, hy_low = hn[r, 0, l - 1], hn[r, 1, l - 1]
            else:
                hx_low = jnp.where(me > 0, below[r, 0] + DT * ey, 0.0)
                hy_low = jnp.where(me > 0, below[r, 1] - DT * ex, 0.0)
            curl = (
                (hz - behind(hz, 1)) - (hy - hy_low),
                (hx - hx_low) - (hz - behind(hz, 0)),
                (hy - behind(hy, 0)) - (hx - behind(hx, 1)),
            )
            fields = (ex, ey, ez)
            result = []
            for c in range(3):
                push = drive[c, rows, :] if r == 0 else seen[rows, :] * e[0, c, l]
                current = (
                    (1.0 - DAMPING * DT / 2.0) * j[r, c, l]
                    + DT * (strength * fields[c] - p[r, c, l])
                ) * (1.0 / (1.0 + DAMPING * DT / 2.0))
                result.append(fields[c] + scale * (curl[c] - current + push))
                en[r, c, l] = result[c]
            store(en.at[r, :, l], (ef_out, ea_out)[r].at[:, l], 0, l, r)
            if r == 0:
                old, new = fields, result
            else:
                product[l] = sum(
                    result[c] * ((new[c] - old[c]) + GAIN_FIELD * new[c]) for c in range(3)
                )
    last = pltpu.make_async_copy(
        product, product_out.at[pl.ds(first_slot, depth)], side_sem.at[3]
    )
    last.start()
    for copy in stores:
        copy.wait()
    last.wait()


def gradient_kernel(
    n,
    depth,
    radius_ref,
    start_ref,
    product_ref,
    grad_ref,
    arrived,
    send_sem,
    recv_sem,
    self_sem,
):
    me = lax.axis_index("gx")
    first, second, shift = holders(me, depth)
    base, low, high = slot_range(me, n, depth)
    barrier = pltpu.get_barrier_semaphore()
    for holder, used in ((first, shift >= 0), (second, shift != 0)):

        @pl.when(used & (holder != me))
        def _():
            pl.semaphore_signal(barrier, inc=1, device_id={"gx": holder}, device_id_type=MESH)

    inside = jnp.where((me >= low) & (me < high), 1, 0)
    count = jnp.maximum(high - low, 0) - inside

    @pl.when(count > 0)
    def _():
        pl.semaphore_wait(barrier, count)

    def back(owner):
        slot = owner - base
        which = jnp.where(slot >= depth - 1, 0, 1)
        return pltpu.make_async_remote_copy(
            src_ref=product_ref.at[slot],
            dst_ref=arrived.at[which],
            send_sem=send_sem.at[slot],
            recv_sem=recv_sem.at[which],
            device_id={"gx": owner},
            device_id_type=MESH,
        )

    def keep():
        slot = me - base
        which = jnp.where(slot >= depth - 1, 0, 1)
        return pltpu.make_async_copy(product_ref.at[slot], arrived.at[which], self_sem)

    @pl.loop(low, high)
    def _(owner):
        pl.when(owner != me)(lambda: back(owner).start())
        pl.when(owner == me)(lambda: keep().start())

    for which, holder, used in ((0, first, shift >= 0), (1, second, shift != 0)):

        @pl.when(used & (holder != me))
        def _():
            pltpu.make_async_remote_copy(
                src_ref=product_ref.at[0],
                dst_ref=arrived.at[which],
                send_sem=send_sem.at[0],
                recv_sem=recv_sem.at[which],
                device_id={"gx": holder},
                device_id_type=MESH,
            ).wait_recv()

        pl.when(used & (holder == me))(lambda: keep().wait())

    radius = radius_ref[0]
    in_first = start_ref[0] + me < (first + 1) * depth
    plane = jnp.where(in_first, arrived[0], arrived[1])
    grad_ref[0] = band_product(plane * inverse_sums(plane.shape, radius), radius)

    @pl.loop(low, high)
    def _(owner):
        pl.when(owner != me)(lambda: back(owner).wait_send())


def body(
    n,
    e_forward,
    h_forward,
    p_forward,
    j_forward,
    e_adjoint,
    h_adjoint,
    p_adjoint,
    j_adjoint,
    design,
    source_amp,
    source_cell,
    monitor_cell,
    slab_start,
    radius,
):
    _, depth, nx, ny = e_forward.shape
    slots = 2 * depth - 1
    dma = pltpu.SemaphoreType.DMA
    below, above, densities = pl.pallas_call(
        functools.partial(exchange_kernel, n),
        out_shape=(
            jax.ShapeDtypeStruct((2, 2, nx, ny), F32),
            jax.ShapeDtypeStruct((2, 2, nx, ny), F32),
            jax.ShapeDtypeStruct((slots, nx, ny), F32),
        ),
        in_specs=[SMEM, VMEM, ANY, ANY, ANY, ANY],
        out_specs=(ANY, ANY, ANY),
        scratch_shapes=[
            pltpu.VMEM((2, 3, nx, ny), F32),
            pltpu.VMEM((2, 2, nx, ny), F32),
            pltpu.VMEM((2, 2, nx, ny), F32),
            pltpu.VMEM((nx, ny), F32),
            dma((2, 2)),
            dma((2,)),
            dma(()),
            dma(()),
            dma((2,)),
            dma((2,)),
            dma((slots,)),
            dma(()),
        ],
        compiler_params=pltpu.CompilerParams(
            collective_id=0, has_side_effects=True, vmem_limit_bytes=6 * 1024 * 1024
        ),
        name="exchange",
    )(radius, design, e_forward, e_adjoint, h_forward, h_adjoint)
    field = jax.ShapeDtypeStruct(e_forward.shape, F32)
    both = pltpu.VMEM((2,) + e_forward.shape, F32)
    ef, hf, ea, ha, product = pl.pallas_call(
        functools.partial(step_kernel, n),
        out_shape=(field, field, field, field, jax.ShapeDtypeStruct((slots, nx, ny), F32)),
        in_specs=[SMEM] * 4 + [ANY] * 11,
        out_specs=(ANY,) * 5,
        scratch_shapes=[
            both,
            both,
            both,
            both,
            pltpu.VMEM((2, 2, nx, ny), F32),
            pltpu.VMEM((2, 2, nx, ny), F32),
            pltpu.VMEM((depth, nx, ny), F32),
            pltpu.VMEM((3, depth * nx, ny), F32),
            pltpu.VMEM((depth * nx, ny), F32),
            pltpu.VMEM((depth, nx, ny), F32),
            both,
            both,
            dma((4, depth, 2)),
            dma((2, depth, 2)),
            dma((4,)),
        ],
        compiler_params=pltpu.CompilerParams(vmem_limit_bytes=24 * 1024 * 1024),
        name="step",
    )(
        slab_start,
        source_amp.T,
        source_cell,
        monitor_cell,
        e_forward,
        h_forward,
        p_forward,
        j_forward,
        e_adjoint,
        h_adjoint,
        p_adjoint,
        j_adjoint,
        below,
        above,
        densities,
    )
    grad = pl.pallas_call(
        functools.partial(gradient_kernel, n, depth),
        out_shape=jax.ShapeDtypeStruct(design.shape, F32),
        in_specs=[SMEM, SMEM, ANY],
        out_specs=VMEM,
        scratch_shapes=[
            pltpu.VMEM((2, nx, ny), F32),
            dma((slots,)),
            dma((2,)),
            dma(()),
        ],
        compiler_params=pltpu.CompilerParams(
            collective_id=1, has_side_effects=True, vmem_limit_bytes=6 * 1024 * 1024
        ),
        name="gradient",
    )(radius, slab_start, product)
    return ef, hf, ea, ha, grad


def solution(mesh):
    field = P(None, ("grp", "gx"), None, None)
    plane = P(("grp", "gx"), None, None)
    return jax.shard_map(
        functools.partial(body, mesh.shape["gx"]),
        mesh=mesh,
        in_specs=(field,) * 8 + (plane, P("grp", None)) + (P("grp"),) * 4,
        out_specs=(field,) * 4 + (plane,),
        check_vma=False,
    )
```

time: 174 us -> 42.1 us (0.24)
  the two profiles are of different devices: /device:TPU:0 before, /device:TPU:25 now
where the time goes in v1:
time: 42.1 us; the launch traced here: 41.5 us
  Pallas kernels  28.4 us (67%)
  local copies, waits for them, and re-layouts  11.1 us (26%)
  between operations  2.03 us (5%)
    pallas_call x1, Pallas kernels, body(): pl.pallas_call(functools.partial(gradient_kernel, n, depth), out_shape=ja...  13.5 us
    unnamed x33, local copies, waits for them, and re-layouts  11.1 us
    pallas_call x1, Pallas kernels, body(): pl.pallas_call(functools.partial(step_kernel, n), out_shape=(field, field...  8.05 us
    pallas_call x1, Pallas kernels, body(): pl.pallas_call(functools.partial(exchange_kernel, n), out_shape=(jax.Shap...  6.89 us

profile of v1, /device:TPU:25, one launch (start us, length us, event | category | flops | bytes accessed | tf_op | source)
XLA Modules:
  0.0 41.5 jit_solution(16090632177052519785)
XLA Ops:
  1.9 0.0 copy-start
  1.9 1.1 %copy-done = f32[3,8,32,256]{3,2,1,0:T(8,128)S(1)} copy-done((f32[3,8,32,256]{3,2,1,0:T(8,128)S(1)}, f32[3,8,32,256]{3,2,1,0:T(8,128)}, u32[]{:S(2)}) %copy-start) | copy-done | bytes 786456
  3.1 1.1 %copy-done.2 = f32[3,8,32,256]{3,2,1,0:T(8,128)S(1)} copy-done((f32[3,8,32,256]{3,2,1,0:T(8,128)S(1)}, f32[3,8,32,256]{3,2,1,0:T(8,128)}, u32[]{:S(2)}) %copy-start.2) | copy-done | bytes 786456
  4.2 1.1 %copy-done.4 = f32[3,8,32,256]{3,2,1,0:T(8,128)S(1)} copy-done((f32[3,8,32,256]{3,2,1,0:T(8,128)S(1)}, f32[3,8,32,256]{3,2,1,0:T(8,128)}, u32[]{:S(2)}) %copy-start.4) | copy-done | bytes 786456
  5.3 1.1 %copy-done.6 = f32[3,8,32,256]{3,2,1,0:T(8,128)S(1)} copy-done((f32[3,8,32,256]{3,2,1,0:T(8,128)S(1)}, f32[3,8,32,256]{3,2,1,0:T(8,128)}, u32[]{:S(2)}) %copy-start.6) | copy-done | bytes 786456
  6.5 0.8 %copy-done.12 = f32[1,32,256]{2,1,0:T(8,128)S(1)} copy-done((f32[1,32,256]{2,1,0:T(8,128)S(1)}, f32[1,32,256]{2,1,0:T(8,128)}, u32[]{:S(2)}) %copy-start.12) | copy-done | bytes 32792
  7.2 6.9 %exchange.1 = (f32[2,2,32,256]{3,2,1,0:T(8,128)S(1)}, f32[2,2,32,256]{3,2,1,0:T(8,128)S(1)}, f32[15,32,256]{2,1,0:T(8,128)S(1)}) custom-call(s32[1]{0:T(128)S(6)} %copy.21.radius_ref, f32[1,32,256]{2,1,0:T(8,128)S(1)} %copy-done.12, f32[3,8,32,256]{3,2,1,0:T(8,128)S(1)} %copy-done, f32[3,8,32,256]{3,2,1,0:T(8,128)S(1)} %copy-done.4, ...), custom_call_target="tpu_custom_call" | custom-call | tf_op jit(solution)/shard_map/exchange/pallas_call | solution.py:487
  14.1 0.0 copy-start.13
  14.1 0.0 copy-start.14
  14.2 0.0 copy-start.15
  14.2 0.0 copy-done.1
  14.2 0.0 copy-done.3
  14.2 0.0 copy-done.5
  14.2 0.0 copy-done.7
  14.2 0.6 %copy-done.13 = f32[16,3]{0,1:T(4,128)S(1)} copy-done((f32[16,3]{0,1:T(4,128)S(1)}, f32[16,3]{0,1:T(4,128)}, u32[]{:S(2)}) %copy-start.13) | copy-done | bytes 216
  14.8 0.0 copy-done.14
  14.8 0.0 copy-done.15
  14.8 1.1 %copy-done.8 = f32[3,8,32,256]{3,2,1,0:T(8,128)S(1)} copy-done((f32[3,8,32,256]{3,2,1,0:T(8,128)S(1)}, f32[3,8,32,256]{3,2,1,0:T(8,128)}, u32[]{:S(2)}) %copy-start.8) | copy-done | bytes 786456
  16.0 1.1 %copy-done.9 = f32[3,8,32,256]{3,2,1,0:T(8,128)S(1)} copy-done((f32[3,8,32,256]{3,2,1,0:T(8,128)S(1)}, f32[3,8,32,256]{3,2,1,0:T(8,128)}, u32[]{:S(2)}) %copy-start.9) | copy-done | bytes 786456
  17.1 1.1 %copy-done.10 = f32[3,8,32,256]{3,2,1,0:T(8,128)S(1)} copy-done((f32[3,8,32,256]{3,2,1,0:T(8,128)S(1)}, f32[3,8,32,256]{3,2,1,0:T(8,128)}, u32[]{:S(2)}) %copy-start.10) | copy-done | bytes 786456
  18.2 1.1 %copy-done.11 = f32[3,8,32,256]{3,2,1,0:T(8,128)S(1)} copy-done((f32[3,8,32,256]{3,2,1,0:T(8,128)S(1)}, f32[3,8,32,256]{3,2,1,0:T(8,128)}, u32[]{:S(2)}) %copy-start.11) | copy-done | bytes 786456
  19.4 8.1 %step.1 = (f32[3,8,32,256]{3,2,1,0:T(8,128)}, f32[3,8,32,256]{3,2,1,0:T(8,128)}, f32[3,8,32,256]{3,2,1,0:T(8,128)}, f32[3,8,32,256]{3,2,1,0:T(8,128)}, f32[15,32,256]{2,1,0:T(8,128)S(1)}) custom-call(s32[1]{0:T(128)S(6)} %copy.20.start_ref, f32[3,16]{1,0:T(4,128)S(1)} %bitcast.1, s32[16]{0:T(128)S(1)} %copy-done.14, s32[16]{0:T(128)S(1)} %copy-done.15, ...), custom_call_target="tpu_custom_call" | custom-call | tf_op jit(solution)/shard_map/step/pallas_call | solution.py:517
  27.4 13.5 %gradient.1 = f32[1,32,256]{2,1,0:T(8,128)S(1)} custom-call(s32[1]{0:T(128)S(6)} %copy.21.radius_ref, s32[1]{0:T(128)S(6)} %copy.20.start_ref, f32[15,32,256]{2,1,0:T(8,128)S(1)} %get-tuple-element.20.product_ref), custom_call_target="tpu_custom_call" | custom-call | tf_op jit(solution)/shard_map/gradient/pallas_call | solution.py:558
  40.9 0.6 %copy.22 = f32[1,32,256]{2,1,0:T(8,128)} copy(f32[1,32,256]{2,1,0:T(8,128)S(1)} %gradient.1) | data formatting | bytes 65536
  (12 shorter events, 0.0 us)
Async XLA Ops:
  1.9 1.1 %copy-start = (f32[3,8,32,256]{3,2,1,0:T(8,128)S(1)}, f32[3,8,32,256]{3,2,1,0:T(8,128)}, u32[]{:S(2)}) copy-start(f32[3,8,32,256]{3,2,1,0:T(8,128)} %ef_in.1) | copy-start | bytes 2359300
  3.1 1.1 %copy-start.2 = (f32[3,8,32,256]{3,2,1,0:T(8,128)S(1)}, f32[3,8,32,256]{3,2,1,0:T(8,128)}, u32[]{:S(2)}) copy-start(f32[3,8,32,256]{3,2,1,0:T(8,128)} %hf_in.1) | copy-start | bytes 2359300
  4.2 1.1 %copy-start.4 = (f32[3,8,32,256]{3,2,1,0:T(8,128)S(1)}, f32[3,8,32,256]{3,2,1,0:T(8,128)}, u32[]{:S(2)}) copy-start(f32[3,8,32,256]{3,2,1,0:T(8,128)} %ea_in.1) | copy-start | bytes 2359300
  5.3 1.1 %copy-start.6 = (f32[3,8,32,256]{3,2,1,0:T(8,128)S(1)}, f32[3,8,32,256]{3,2,1,0:T(8,128)}, u32[]{:S(2)}) copy-start(f32[3,8,32,256]{3,2,1,0:T(8,128)} %ha_in.1) | copy-start | bytes 2359300
  6.5 0.8 %copy-start.12 = (f32[1,32,256]{2,1,0:T(8,128)S(1)}, f32[1,32,256]{2,1,0:T(8,128)}, u32[]{:S(2)}) copy-start(f32[1,32,256]{2,1,0:T(8,128)} %design_ref.1) | copy-start | bytes 98308
  7.2 6.9 %copy-start.1 = (f32[3,8,32,256]{3,2,1,0:T(8,128)S(1)}, f32[3,8,32,256]{3,2,1,0:T(8,128)}, u32[]{:S(2)}) copy-start(f32[3,8,32,256]{3,2,1,0:T(8,128)} %ef_in.1) | copy-start | bytes 2359300
  7.2 7.0 %copy-start.3 = (f32[3,8,32,256]{3,2,1,0:T(8,128)S(1)}, f32[3,8,32,256]{3,2,1,0:T(8,128)}, u32[]{:S(2)}) copy-start(f32[3,8,32,256]{3,2,1,0:T(8,128)} %hf_in.1) | copy-start | bytes 2359300
  7.2 7.0 %copy-start.5 = (f32[3,8,32,256]{3,2,1,0:T(8,128)S(1)}, f32[3,8,32,256]{3,2,1,0:T(8,128)}, u32[]{:S(2)}) copy-start(f32[3,8,32,256]{3,2,1,0:T(8,128)} %ea_in.1) | copy-start | bytes 2359300
  7.2 7.0 %copy-start.7 = (f32[3,8,32,256]{3,2,1,0:T(8,128)S(1)}, f32[3,8,32,256]{3,2,1,0:T(8,128)}, u32[]{:S(2)}) copy-start(f32[3,8,32,256]{3,2,1,0:T(8,128)} %ha_in.1) | copy-start | bytes 2359300
  14.1 0.7 %copy-start.13 = (f32[16,3]{0,1:T(4,128)S(1)}, f32[16,3]{0,1:T(4,128)}, u32[]{:S(2)}) copy-start(f32[16,3]{0,1:T(4,128)} %param.23) | copy-start | bytes 580
  14.1 0.7 %copy-start.14 = (s32[16]{0:T(128)S(1)}, s32[16]{0:T(128)}, u32[]{:S(2)}) copy-start(s32[16]{0:T(128)} %source_ref.1) | copy-start | bytes 196
  14.2 0.7 %copy-start.15 = (s32[16]{0:T(128)S(1)}, s32[16]{0:T(128)}, u32[]{:S(2)}) copy-start(s32[16]{0:T(128)} %monitor_ref.1) | copy-start | bytes 196
  14.8 1.1 %copy-start.8 = (f32[3,8,32,256]{3,2,1,0:T(8,128)S(1)}, f32[3,8,32,256]{3,2,1,0:T(8,128)}, u32[]{:S(2)}) copy-start(f32[3,8,32,256]{3,2,1,0:T(8,128)} %pf_in.1) | copy-start | bytes 2359300
  16.0 1.1 %copy-start.9 = (f32[3,8,32,256]{3,2,1,0:T(8,128)S(1)}, f32[3,8,32,256]{3,2,1,0:T(8,128)}, u32[]{:S(2)}) copy-start(f32[3,8,32,256]{3,2,1,0:T(8,128)} %jf_in.1) | copy-start | bytes 2359300
  17.1 1.1 %copy-start.10 = (f32[3,8,32,256]{3,2,1,0:T(8,128)S(1)}, f32[3,8,32,256]{3,2,1,0:T(8,128)}, u32[]{:S(2)}) copy-start(f32[3,8,32,256]{3,2,1,0:T(8,128)} %pa_in.1) | copy-start | bytes 2359300
  18.2 1.1 %copy-start.11 = (f32[3,8,32,256]{3,2,1,0:T(8,128)S(1)}, f32[3,8,32,256]{3,2,1,0:T(8,128)}, u32[]{:S(2)}) copy-start(f32[3,8,32,256]{3,2,1,0:T(8,128)} %ja_in.1) | copy-start | bytes 2359300

commit v2 on v1

--- a/solution.py
+++ b/solution.py
@@ -13,10 +13,11 @@
 STRENGTH_RANGE = 3.0
 DAMPING = 0.2
 GAIN_FIELD = 0.25
+BIG = 60 * 1024 * 1024
 MESH = pl.DeviceIdType.MESH
 F32 = jnp.float32
 BF16 = jnp.bfloat16
-ANY = pl.BlockSpec(memory_space=pl.ANY)
+HBM = pl.BlockSpec(memory_space=pltpu.HBM)
 SMEM = pl.BlockSpec(memory_space=pltpu.SMEM)
 VMEM = pl.BlockSpec(memory_space=pltpu.VMEM)
 
@@ -491,8 +492,8 @@
             jax.ShapeDtypeStruct((2, 2, nx, ny), F32),
             jax.ShapeDtypeStruct((slots, nx, ny), F32),
         ),
-        in_specs=[SMEM, VMEM, ANY, ANY, ANY, ANY],
-        out_specs=(ANY, ANY, ANY),
+        in_specs=[SMEM, VMEM, HBM, HBM, HBM, HBM],
+        out_specs=(HBM, HBM, HBM),
         scratch_shapes=[
             pltpu.VMEM((2, 3, nx, ny), F32),
             pltpu.VMEM((2, 2, nx, ny), F32),
@@ -508,7 +509,7 @@
             dma(()),
         ],
         compiler_params=pltpu.CompilerParams(
-            collective_id=0, has_side_effects=True, vmem_limit_bytes=6 * 1024 * 1024
+            collective_id=0, has_side_effects=True, vmem_limit_bytes=BIG
         ),
         name="exchange",
     )(radius, design, e_forward, e_adjoint, h_forward, h_adjoint)
@@ -517,8 +518,8 @@
     ef, hf, ea, ha, product = pl.pallas_call(
         functools.partial(step_kernel, n),
         out_shape=(field, field, field, field, jax.ShapeDtypeStruct((slots, nx, ny), F32)),
-        in_specs=[SMEM] * 4 + [ANY] * 11,
-        out_specs=(ANY,) * 5,
+        in_specs=[SMEM] * 4 + [HBM] * 11,
+        out_specs=(HBM,) * 5,
         scratch_shapes=[
             both,
             both,
@@ -536,7 +537,7 @@
             dma((2, depth, 2)),
             dma((4,)),
         ],
-        compiler_params=pltpu.CompilerParams(vmem_limit_bytes=24 * 1024 * 1024),
+        compiler_params=pltpu.CompilerParams(vmem_limit_bytes=BIG),
         name="step",
     )(
         slab_start,
@@ -558,7 +559,7 @@
     grad = pl.pallas_call(
         functools.partial(gradient_kernel, n, depth),
         out_shape=jax.ShapeDtypeStruct(design.shape, F32),
-        in_specs=[SMEM, SMEM, ANY],
+        in_specs=[SMEM, SMEM, HBM],
         out_specs=VMEM,
         scratch_shapes=[
             pltpu.VMEM((2, nx, ny), F32),
@@ -567,7 +568,7 @@
             dma(()),
         ],
         compiler_params=pltpu.CompilerParams(
-            collective_id=1, has_side_effects=True, vmem_limit_bytes=6 * 1024 * 1024
+            collective_id=1, has_side_effects=True, vmem_limit_bytes=BIG
         ),
         name="gradient",
     )(radius, slab_start, product)

time: 42.1 us -> 32.8 us (0.78)
  local copies, waits for them, and re-layouts: 11.1 us -> 1.38 us
  Pallas kernels: 28.4 us -> 29.2 us
    unnamed x33 -> x1, local copies, waits for them, and re-layouts: 11.1 us -> 1.38 us
    pallas_call x1, Pallas kernels: 6.89 us -> 7.71 us  [body(): pl.pallas_call(functools.partial(exchange_kernel, n), out_shape=(jax.Shap...]
    pallas_call x1, Pallas kernels: 8.05 us -> 7.42 us  [body(): pl.pallas_call(functools.partial(step_kernel, n), out_shape=(field, field...]
    pallas_call x1, Pallas kernels: 13.5 us -> 14 us  [body(): pl.pallas_call(functools.partial(gradient_kernel, n, depth), out_shape=ja...]
where the time goes in v2:
time: 32.8 us; the launch traced here: 32.5 us
  Pallas kernels  29.2 us (89%)
  between operations  1.95 us (6%)
  local copies, waits for them, and re-layouts  1.38 us (4%)
    pallas_call x1, Pallas kernels, body(): pl.pallas_call(functools.partial(gradient_kernel, n, depth), out_shape=ja...  14 us
    pallas_call x1, Pallas kernels, body(): pl.pallas_call(functools.partial(exchange_kernel, n), out_shape=(jax.Shap...  7.71 us
    pallas_call x1, Pallas kernels, body(): pl.pallas_call(functools.partial(step_kernel, n), out_shape=(field, field...  7.42 us
    unnamed x1, local copies, waits for them, and re-layouts  1.38 us

profile of v2, /device:TPU:25, one launch (start us, length us, event | category | flops | bytes accessed | tf_op | source)
XLA Modules:
  0.0 32.5 jit_solution(7680523697108912275)
XLA Ops:
  1.9 7.7 %exchange.1 = (f32[2,2,32,256]{3,2,1,0:T(8,128)}, f32[2,2,32,256]{3,2,1,0:T(8,128)}, f32[15,32,256]{2,1,0:T(8,128)}) custom-call(s32[1]{0:T(128)S(6)} %copy.21.radius_ref, f32[1,32,256]{2,1,0:T(8,128)} %design_ref.1, f32[3,8,32,256]{3,2,1,0:T(8,128)} %ef_in.1, f32[3,8,32,256]{3,2,1,0:T(8,128)} %ea_in.1, f32[3,8,32,256]{3,2,1,0:T(8,128)} %hf_in.1, ...), custom_call_target="tpu_custom_call" | custom-call | tf_op jit(solution)/shard_map/exchange/pallas_call | solution.py:488
  9.6 7.4 %step.1 = (f32[3,8,32,256]{3,2,1,0:T(8,128)}, f32[3,8,32,256]{3,2,1,0:T(8,128)}, f32[3,8,32,256]{3,2,1,0:T(8,128)}, f32[3,8,32,256]{3,2,1,0:T(8,128)}, f32[15,32,256]{2,1,0:T(8,128)}) custom-call(s32[1]{0:T(128)S(6)} %copy.20.start_ref, f32[3,16]{1,0:T(4,128)} %bitcast.1, s32[16]{0:T(128)} %source_ref.1, s32[16]{0:T(128)} %monitor_ref.1, ...), custom_call_target="tpu_custom_call" | custom-call | tf_op jit(solution)/shard_map/step/pallas_call | solution.py:518
  17.1 14.0 %gradient.1 = f32[1,32,256]{2,1,0:T(8,128)} custom-call(s32[1]{0:T(128)S(6)} %copy.21.radius_ref, s32[1]{0:T(128)S(6)} %copy.20.start_ref, f32[15,32,256]{2,1,0:T(8,128)} %get-tuple-element.20.product_ref), custom_call_target="tpu_custom_call" | custom-call | tf_op jit(solution)/shard_map/gradient/pallas_call | solution.py:559
  31.1 1.4 %copy.22 = f32[1,32,256]{2,1,0:T(8,128)} copy(f32[1,32,256]{2,1,0:T(8,128)} %gradient.1) | data formatting | bytes 65536

commit v3 on v2

--- a/solution.py
+++ b/solution.py
@@ -20,16 +20,6 @@
 HBM = pl.BlockSpec(memory_space=pltpu.HBM)
 SMEM = pl.BlockSpec(memory_space=pltpu.SMEM)
 VMEM = pl.BlockSpec(memory_space=pltpu.VMEM)
-
-
-def slot_range(me, n, depth):
-    base = depth * (me - 1) - (depth - 1)
-    return base, jnp.maximum(base, 0), jnp.minimum(base + 2 * depth - 1, n)
-
-
-def holders(me, depth):
-    first = me // depth + 1
-    return first, first + 1, me % depth
 
 
 def ahead(v, axis):
@@ -95,6 +85,7 @@
     rho,
     load_sem,
     send_sem,
+    onward_send,
     up_send,
     up_recv,
     down_send,
@@ -124,27 +115,41 @@
     rho[...] = band_product(plane, radius) * inverse_sums(plane.shape, radius)
     pl.semaphore_wait(barrier, n - 1)
 
-    first, second, shift = holders(me, depth)
-
-    def to_holder(which, holder):
-        slot = me - (depth * (holder - 1) - (depth - 1))
+    first = me // depth + 1
+
+    def to_holder():
+        slot = me % depth + depth - 1
         return pltpu.make_async_remote_copy(
             src_ref=rho,
             dst_ref=slots_ref.at[slot],
-            send_sem=send_sem.at[which],
+            send_sem=send_sem,
             recv_sem=slot_recv.at[slot],
-            device_id={"gx": holder},
+            device_id={"gx": first},
             device_id_type=MESH,
         )
 
-    def to_self(holder):
-        slot = me - (depth * (holder - 1) - (depth - 1))
-        return pltpu.make_async_copy(rho, slots_ref.at[slot], self_sem)
-
-    def each_holder(remote, local):
-        for which, holder, used in ((0, first, shift >= 0), (1, second, shift != 0)):
-            pl.when(used & (holder != me))(functools.partial(remote, which, holder))
-            pl.when(used & (holder == me))(functools.partial(local, holder))
+    def to_self():
+        return pltpu.make_async_copy(rho, slots_ref.at[me % depth + depth - 1], self_sem)
+
+    def onward(k):
+        return pltpu.make_async_remote_copy(
+            src_ref=slots_ref.at[depth - 1 + k],
+            dst_ref=slots_ref.at[k - 1],
+            send_sem=onward_send.at[k],
+            recv_sem=slot_recv.at[k - 1],
+            device_id={"gx": me + 1},
+            device_id_type=MESH,
+        )
+
+    def landed(slot):
+        return pltpu.make_async_remote_copy(
+            src_ref=rho,
+            dst_ref=slots_ref.at[slot],
+            send_sem=send_sem,
+            recv_sem=slot_recv.at[slot],
+            device_id={"gx": first},
+            device_id_type=MESH,
+        )
 
     def to_below(r, e):
         return pltpu.make_async_remote_copy(
@@ -166,10 +171,8 @@
             device_id_type=MESH,
         )
 
-    each_holder(
-        lambda which, holder: to_holder(which, holder).start(),
-        lambda holder: to_self(holder).start(),
-    )
+    pl.when(first != me)(lambda: to_holder().start())
+    pl.when(first == me)(lambda: to_self().start())
 
     @pl.when(me > 0)
     def _():
@@ -187,10 +190,14 @@
     def _():
         to_above().start()
 
-    each_holder(
-        lambda which, holder: to_holder(which, holder).wait_send(),
-        lambda holder: to_self(holder).wait(),
-    )
+    @pl.when((me >= 1) & (depth * (me - 1) < n))
+    def _():
+        @pl.loop(0, depth)
+        def _(k):
+            owner = depth * (me - 1) + k
+            pl.when((owner < n) & (owner != me))(lambda: landed(depth - 1 + k).wait_recv())
+            pl.when(owner == me)(lambda: to_self().wait())
+            pl.when((owner < n) & (k > 0))(lambda: onward(k).start())
 
     @pl.when(me > 0)
     def _():
@@ -204,20 +211,19 @@
         to_below(0, ef).wait_recv()
         to_below(1, ea).wait_recv()
 
-    base, low, high = slot_range(me, n, depth)
-
-    @pl.loop(low, high)
-    def _(owner):
-        @pl.when(owner != me)
-        def _():
-            pltpu.make_async_remote_copy(
-                src_ref=rho,
-                dst_ref=slots_ref.at[owner - base],
-                send_sem=send_sem.at[0],
-                recv_sem=slot_recv.at[owner - base],
-                device_id={"gx": owner},
-                device_id_type=MESH,
-            ).wait_recv()
+    pl.when(first != me)(lambda: to_holder().wait_send())
+
+    @pl.when((me >= 2) & (depth * (me - 2) < n))
+    def _():
+        @pl.loop(1, depth)
+        def _(k):
+            pl.when(depth * (me - 2) + k < n)(lambda: landed(k - 1).wait_recv())
+
+    @pl.when((me >= 1) & (depth * (me - 1) < n))
+    def _():
+        @pl.loop(1, depth)
+        def _(k):
+            pl.when(depth * (me - 1) + k < n)(lambda: onward(k).wait_send())
 
 
 def step_kernel(
@@ -397,72 +403,101 @@
     product_ref,
     grad_ref,
     arrived,
+    own,
+    relayed,
+    load_sem,
+    relay_send,
+    relay_recv,
     send_sem,
     recv_sem,
     self_sem,
 ):
     me = lax.axis_index("gx")
-    first, second, shift = holders(me, depth)
-    base, low, high = slot_range(me, n, depth)
+    first = me // depth + 1
+    base = depth * (me - 1)
+    is_first = (me >= 1) & (base < n)
+    is_second = (me >= 2) & (base - depth < n)
+    load = pltpu.make_async_copy(product_ref.at[pl.ds(depth - 1, depth)], own, load_sem)
+    pl.when(is_first)(lambda: load.start())
+
     barrier = pltpu.get_barrier_semaphore()
-    for holder, used in ((first, shift >= 0), (second, shift != 0)):
-
-        @pl.when(used & (holder != me))
-        def _():
-            pl.semaphore_signal(barrier, inc=1, device_id={"gx": holder}, device_id_type=MESH)
-
-    inside = jnp.where((me >= low) & (me < high), 1, 0)
-    count = jnp.maximum(high - low, 0) - inside
-
-    @pl.when(count > 0)
-    def _():
-        pl.semaphore_wait(barrier, count)
-
-    def back(owner):
-        slot = owner - base
-        which = jnp.where(slot >= depth - 1, 0, 1)
+
+    def signal(device):
+        pl.semaphore_signal(barrier, inc=1, device_id={"gx": device}, device_id_type=MESH)
+
+    pl.when(first != me)(lambda: signal(first))
+    pl.when(is_first)(lambda: signal(me + 1))
+    owners = jnp.where(is_first, jnp.minimum(n - base, depth), 0)
+    owners -= jnp.where(first == me, 1, 0)
+    count = owners + jnp.where(is_second, 1, 0)
+    pl.when(count > 0)(lambda: pl.semaphore_wait(barrier, count))
+
+    def relay(k):
         return pltpu.make_async_remote_copy(
-            src_ref=product_ref.at[slot],
-            dst_ref=arrived.at[which],
-            send_sem=send_sem.at[slot],
-            recv_sem=recv_sem.at[which],
-            device_id={"gx": owner},
+            src_ref=product_ref.at[k - 1],
+            dst_ref=relayed.at[k],
+            send_sem=relay_send.at[k],
+            recv_sem=relay_recv.at[k],
+            device_id={"gx": me - 1},
             device_id_type=MESH,
         )
 
-    def keep():
-        slot = me - base
-        which = jnp.where(slot >= depth - 1, 0, 1)
-        return pltpu.make_async_copy(product_ref.at[slot], arrived.at[which], self_sem)
-
-    @pl.loop(low, high)
-    def _(owner):
-        pl.when(owner != me)(lambda: back(owner).start())
-        pl.when(owner == me)(lambda: keep().start())
-
-    for which, holder, used in ((0, first, shift >= 0), (1, second, shift != 0)):
-
-        @pl.when(used & (holder != me))
-        def _():
-            pltpu.make_async_remote_copy(
-                src_ref=product_ref.at[0],
-                dst_ref=arrived.at[which],
-                send_sem=send_sem.at[0],
-                recv_sem=recv_sem.at[which],
-                device_id={"gx": holder},
-                device_id_type=MESH,
-            ).wait_recv()
-
-        pl.when(used & (holder == me))(lambda: keep().wait())
+    def back(k):
+        return pltpu.make_async_remote_copy(
+            src_ref=own.at[k],
+            dst_ref=arrived,
+            send_sem=send_sem.at[k],
+            recv_sem=recv_sem,
+            device_id={"gx": base + k},
+            device_id_type=MESH,
+        )
+
+    def keep(k):
+        return pltpu.make_async_copy(own.at[k], arrived, self_sem)
+
+    @pl.when(is_second)
+    def _():
+        @pl.loop(1, depth)
+        def _(k):
+            pl.when(base - depth + k < n)(lambda: relay(k).start())
+
+    @pl.when(is_first)
+    def _():
+        load.wait()
+        for k in range(depth):
+
+            @pl.when(base + k < n)
+            def _():
+                if k:
+                    relay(k).wait_recv()
+                    here = start_ref[0] + base + k < (me + 1) * depth
+                    own[k] = jnp.where(here, own[k], relayed[k])
+                pl.when(base + k != me)(lambda: back(k).start())
+                pl.when(base + k == me)(lambda: keep(k).start())
+
+    @pl.when(first != me)
+    def _():
+        back(0).wait_recv()
+
+    @pl.when(first == me)
+    def _():
+        keep(0).wait()
 
     radius = radius_ref[0]
-    in_first = start_ref[0] + me < (first + 1) * depth
-    plane = jnp.where(in_first, arrived[0], arrived[1])
+    plane = arrived[...]
     grad_ref[0] = band_product(plane * inverse_sums(plane.shape, radius), radius)
 
-    @pl.loop(low, high)
-    def _(owner):
-        pl.when(owner != me)(lambda: back(owner).wait_send())
+    @pl.when(is_second)
+    def _():
+        @pl.loop(1, depth)
+        def _(k):
+            pl.when(base - depth + k < n)(lambda: relay(k).wait_send())
+
+    @pl.when(is_first)
+    def _():
+        @pl.loop(0, depth)
+        def _(k):
+            pl.when((base + k < n) & (base + k != me))(lambda: back(k).wait_send())
 
 
 def body(
@@ -500,7 +535,8 @@
             pltpu.VMEM((2, 2, nx, ny), F32),
             pltpu.VMEM((nx, ny), F32),
             dma((2, 2)),
-            dma((2,)),
+            dma(()),
+            dma((depth,)),
             dma(()),
             dma(()),
             dma((2,)),
@@ -562,9 +598,14 @@
         in_specs=[SMEM, SMEM, HBM],
         out_specs=VMEM,
         scratch_shapes=[
-            pltpu.VMEM((2, nx, ny), F32),
-            dma((slots,)),
-            dma((2,)),
+            pltpu.VMEM((nx, ny), F32),
+            pltpu.VMEM((depth, nx, ny), F32),
+            pltpu.VMEM((depth, nx, ny), F32),
+            dma(()),
+            dma((depth,)),
+            dma((depth,)),
+            dma((depth,)),
+            dma(()),
             dma(()),
         ],
         compiler_params=pltpu.CompilerParams(

time: 32.8 us -> 33.6 us (1.024)
  the two profiles are of different devices: /device:TPU:25 before, /device:TPU:1 now
where the time goes in v3:
time: 33.6 us; the launch traced here: 33.3 us
  Pallas kernels  30 us (89%)
  between operations  1.95 us (6%)
  local copies, waits for them, and re-layouts  1.38 us (4%)
    pallas_call x1, Pallas kernels, body(): pl.pallas_call(functools.partial(exchange_kernel, n), out_shape=(jax.Shap...  14.2 us
    pallas_call x1, Pallas kernels, body(): pl.pallas_call(functools.partial(gradient_kernel, n, depth), out_shape=ja...  8.36 us
    pallas_call x1, Pallas kernels, body(): pl.pallas_call(functools.partial(step_kernel, n), out_shape=(field, field...  7.42 us
    unnamed x1, local copies, waits for them, and re-layouts  1.38 us

profile of v3, /device:TPU:1, one launch (start us, length us, event | category | flops | bytes accessed | tf_op | source)
XLA Modules:
  0.0 33.3 jit_solution(7852168839448014330)
XLA Ops:
  1.9 14.2 %exchange.1 = (f32[2,2,32,256]{3,2,1,0:T(8,128)}, f32[2,2,32,256]{3,2,1,0:T(8,128)}, f32[15,32,256]{2,1,0:T(8,128)}) custom-call(s32[1]{0:T(128)S(6)} %copy.21.radius_ref, f32[1,32,256]{2,1,0:T(8,128)} %design_ref.1, f32[3,8,32,256]{3,2,1,0:T(8,128)} %ef_in.1, f32[3,8,32,256]{3,2,1,0:T(8,128)} %ea_in.1, f32[3,8,32,256]{3,2,1,0:T(8,128)} %hf_in.1, ...), custom_call_target="tpu_custom_call" | custom-call | tf_op jit(solution)/shard_map/exchange/pallas_call | solution.py:523
  16.1 7.4 %step.1 = (f32[3,8,32,256]{3,2,1,0:T(8,128)}, f32[3,8,32,256]{3,2,1,0:T(8,128)}, f32[3,8,32,256]{3,2,1,0:T(8,128)}, f32[3,8,32,256]{3,2,1,0:T(8,128)}, f32[15,32,256]{2,1,0:T(8,128)}) custom-call(s32[1]{0:T(128)S(6)} %copy.20.start_ref, f32[3,16]{1,0:T(4,128)} %bitcast.1, s32[16]{0:T(128)} %source_ref.1, s32[16]{0:T(128)} %monitor_ref.1, ...), custom_call_target="tpu_custom_call" | custom-call | tf_op jit(solution)/shard_map/step/pallas_call | solution.py:554
  23.5 8.4 %gradient.1 = f32[1,32,256]{2,1,0:T(8,128)} custom-call(s32[1]{0:T(128)S(6)} %copy.21.radius_ref, s32[1]{0:T(128)S(6)} %copy.20.start_ref, f32[15,32,256]{2,1,0:T(8,128)} %get-tuple-element.20.product_ref), custom_call_target="tpu_custom_call" | custom-call | tf_op jit(solution)/shard_map/gradient/pallas_call | solution.py:595
  31.9 1.4 %copy.22 = f32[1,32,256]{2,1,0:T(8,128)} copy(f32[1,32,256]{2,1,0:T(8,128)} %gradient.1) | data formatting | bytes 65536

commit v4 on v2

--- a/solution.py
+++ b/solution.py
@@ -14,6 +14,8 @@
 DAMPING = 0.2
 GAIN_FIELD = 0.25
 BIG = 60 * 1024 * 1024
+SMALL = 6 * 1024 * 1024
+CHUNK = 2
 MESH = pl.DeviceIdType.MESH
 F32 = jnp.float32
 BF16 = jnp.bfloat16
@@ -269,18 +271,19 @@
     ]
     loads = {}
     pairs = ((e, ef_in, ea_in), (h, hf_in, ha_in), (j, jf_in, ja_in), (p, pf_in, pa_in))
-    for l in range(depth):
+    for l in range(0, depth, CHUNK):
+        part = pl.ds(l, CHUNK)
         for k, (ref, *sources) in enumerate(pairs):
             for r, source in enumerate(sources):
                 loads[k, l, r] = pltpu.make_async_copy(
-                    source.at[:, l], ref.at[r, :, l], in_sem.at[k, l, r]
+                    source.at[:, part], ref.at[r, :, part], in_sem.at[k, l, r]
                 )
     for r in range(2):
         loads[0, 0, r].start()
-    for l in range(depth):
+    for l in range(0, depth, CHUNK):
         for r in range(2):
-            if l + 1 < depth:
-                loads[0, l + 1, r].start()
+            if l + CHUNK < depth:
+                loads[0, l + CHUNK, r].start()
             for k in (1, 2, 3):
                 loads[k, l, r].start()
         if l == 0:
@@ -324,10 +327,11 @@
         loads[0, 0, r].wait()
     for l in range(depth):
         for r in range(2):
-            if l + 1 < depth:
+            if (0, l + 1, r) in loads:
                 loads[0, l + 1, r].wait()
             for k in (1, 2, 3):
-                loads[k, l, r].wait()
+                if (k, l, r) in loads:
+                    loads[k, l, r].wait()
         if l == 0:
             sides[0].wait()
             sides[1].wait()
@@ -352,7 +356,9 @@
             hn[r, 0, l] = hx
             hn[r, 1, l] = hy
             hn[r, 2, l] = hz
-            store(hn.at[r, :, l], (hf_out, ha_out)[r].at[:, l], 1, l, r)
+            done = pl.ds(l - CHUNK + 1, CHUNK)
+            if (l + 1) % CHUNK == 0:
+                store(hn.at[r, :, done], (hf_out, ha_out)[r].at[:, done], 1, l, r)
             if l:
                 hx_low, hy_low = hn[r, 0, l - 1], hn[r, 1, l - 1]
             else:
@@ -373,7 +379,8 @@
                 ) * (1.0 / (1.0 + DAMPING * DT / 2.0))
                 result.append(fields[c] + scale * (curl[c] - current + push))
                 en[r, c, l] = result[c]
-            store(en.at[r, :, l], (ef_out, ea_out)[r].at[:, l], 0, l, r)
+            if (l + 1) % CHUNK == 0:
+                store(en.at[r, :, done], (ef_out, ea_out)[r].at[:, done], 0, l, r)
             if r == 0:
                 old, new = fields, result
             else:
@@ -568,7 +575,7 @@
             dma(()),
         ],
         compiler_params=pltpu.CompilerParams(
-            collective_id=1, has_side_effects=True, vmem_limit_bytes=BIG
+            collective_id=1, has_side_effects=True, vmem_limit_bytes=SMALL
         ),
         name="gradient",
     )(radius, slab_start, product)

time: 32.8 us -> 32.1 us (0.979)
  Pallas kernels: 29.2 us -> 28.2 us
    pallas_call x1, Pallas kernels: 14 us -> 13.1 us  [body(): pl.pallas_call(functools.partial(gradient_kernel, n, depth), out_shape=ja...]
    unnamed x1 -> x3, local copies, waits for them, and re-layouts: 1.38 us -> 1.64 us
where the time goes in v4:
time: 32.1 us; the launch traced here: 31.8 us
  Pallas kernels  28.2 us (88%)
  between operations  1.96 us (6%)
  local copies, waits for them, and re-layouts  1.64 us (5%)
    pallas_call x1, Pallas kernels, body(): pl.pallas_call(functools.partial(gradient_kernel, n, depth), out_shape=ja...  13.1 us
    pallas_call x1, Pallas kernels, body(): pl.pallas_call(functools.partial(exchange_kernel, n), out_shape=(jax.Shap...  7.71 us
    pallas_call x1, Pallas kernels, body(): pl.pallas_call(functools.partial(step_kernel, n), out_shape=(field, field...  7.35 us
    unnamed x3, local copies, waits for them, and re-layouts  1.64 us

profile of v4, /device:TPU:25, one launch (start us, length us, event | category | flops | bytes accessed | tf_op | source)
XLA Modules:
  0.0 31.8 jit_solution(3163455279266879200)
XLA Ops:
  1.9 7.7 %exchange.1 = (f32[2,2,32,256]{3,2,1,0:T(8,128)}, f32[2,2,32,256]{3,2,1,0:T(8,128)}, f32[15,32,256]{2,1,0:T(8,128)}) custom-call(s32[1]{0:T(128)S(6)} %copy.21.radius_ref, f32[1,32,256]{2,1,0:T(8,128)} %design_ref.1, f32[3,8,32,256]{3,2,1,0:T(8,128)} %ef_in.1, f32[3,8,32,256]{3,2,1,0:T(8,128)} %ea_in.1, f32[3,8,32,256]{3,2,1,0:T(8,128)} %hf_in.1, ...), custom_call_target="tpu_custom_call" | custom-call | tf_op jit(solution)/shard_map/exchange/pallas_call | solution.py:495
  9.6 7.3 %step.1 = (f32[3,8,32,256]{3,2,1,0:T(8,128)}, f32[3,8,32,256]{3,2,1,0:T(8,128)}, f32[3,8,32,256]{3,2,1,0:T(8,128)}, f32[3,8,32,256]{3,2,1,0:T(8,128)}, f32[15,32,256]{2,1,0:T(8,128)}) custom-call(s32[1]{0:T(128)S(6)} %copy.20.start_ref, f32[3,16]{1,0:T(4,128)} %bitcast.1, s32[16]{0:T(128)} %source_ref.1, s32[16]{0:T(128)} %monitor_ref.1, ...), custom_call_target="tpu_custom_call" | custom-call | tf_op jit(solution)/shard_map/step/pallas_call | solution.py:525
  17.0 0.0 copy-start
  17.0 1.0 %copy-done = f32[15,32,256]{2,1,0:T(8,128)S(1)} copy-done((f32[15,32,256]{2,1,0:T(8,128)S(1)}, f32[15,32,256]{2,1,0:T(8,128)}, u32[]{:S(2)}) %copy-start) | copy-done | bytes 491544
  18.0 13.1 %gradient.1 = f32[1,32,256]{2,1,0:T(8,128)S(1)} custom-call(s32[1]{0:T(128)S(6)} %copy.21.radius_ref, s32[1]{0:T(128)S(6)} %copy.20.start_ref, f32[15,32,256]{2,1,0:T(8,128)S(1)} %copy-done), custom_call_target="tpu_custom_call" | custom-call | tf_op jit(solution)/shard_map/gradient/pallas_call | solution.py:566
  31.2 0.6 %copy.22 = f32[1,32,256]{2,1,0:T(8,128)} copy(f32[1,32,256]{2,1,0:T(8,128)S(1)} %gradient.1) | data formatting | bytes 65536
Async XLA Ops:
  17.0 1.0 %copy-start = (f32[15,32,256]{2,1,0:T(8,128)S(1)}, f32[15,32,256]{2,1,0:T(8,128)}, u32[]{:S(2)}) copy-start(f32[15,32,256]{2,1,0:T(8,128)} %get-tuple-element.20.product_ref) | copy-start | bytes 1474564
